TPU v7x, 512 devices: a whole 4x4x16 slice. The times are simulated.
512 devices in a mesh: seq: 64 (over z, x), tp: 8 (over y, core).
Axes of the slice: x: 4, y: 4, z: 16, core: 2. Of those that a mesh axis runs over, the one named last changes fastest.
Arguments:
- x_in: bfloat16 [8192, 8192], P('seq', 'tp'), may hold values from -6 to 6
- bc_in: bfloat16 [8192, 2, 2048], P('seq', None, 'tp'), may hold values from -3 to 3
- z_in: bfloat16 [8192, 8192], P('seq', 'tp'), may hold values from -6 to 6
- dt_raw: bfloat16 [8192, 128], P('seq', 'tp'), may hold values from -5 to 5
- starts: int32 [8192], P('seq'), may hold values 0 or 1
- conv_x: float32 [4, 8192], P(None, 'tp'), may hold values from -3 to 3
- conv_bc: float32 [4, 2, 2048], P(None, None, 'tp'), may hold values from -3 to 3
- a_log: float32 [128], P('tp'), may hold values from -9 to -3
- dt_bias: float32 [128], P('tp'), may hold values from -2 to 1
- d_skip: float32 [128], P('tp'), may hold values from 0.5 to 2
- norm_gain: float32 [8192], P('tp'), may hold values from 0.5 to 1.5
Outputs:
- mixed: bfloat16 [8192, 8192], P('seq', 'tp')
All inputs are finite; a program needn't handle non-finite values. No bound on the sum of `starts` on one device may be relied on, other than what follows from the above.
Results may differ from a plain program's by a relative error of at most 0.0085.
Values may be sent and summed in bfloat16 or wider, within the bound.
A program may use at most 192 MiB of HBM per device.

v0:
```python
import functools

import jax
import jax.numpy as jnp
from jax import lax
from jax.experimental import pallas as pl
from jax.experimental.pallas import tpu as pltpu
from jax.sharding import PartitionSpec as P

NX = 4
GROUP = 4
CHUNKS = 2
HEAD = 16
REACH = 3
FOLD = 4
EPSILON = 1e-05
MESH = pl.DeviceIdType.MESH
F32, BF16 = jnp.float32, jnp.bfloat16


def dot(a, b):
    return jnp.dot(a, b, preferred_element_type=F32)


def dot_nt(a, b):
    return lax.dot_general(a, b, (((1,), (1,)), ((), ())), preferred_element_type=F32)


def dot_tn(a, b):
    return lax.dot_general(a, b, (((0,), (0,)), ((), ())), preferred_element_type=F32)


def iota(shape, axis):
    return lax.broadcasted_iota(jnp.int32, shape, axis)


def pieces(value, count):
    parts = []
    for _ in range(count):
        part = value.astype(BF16)
        parts.append(part)
        value = value - part.astype(F32)
    return jnp.concatenate(parts, axis=0)


def silu(value):
    return value * jax.nn.sigmoid(value)


def kernel(
    nz, nx, ntp,
    x_hbm, bc_hbm, z_hbm, dt_hbm, st_hbm, cx_hbm, cbc_hbm, al_hbm, db_hbm, ds_hbm, ng_hbm,
    out_ref,
    x_ref, bc_ref, z_ref, dt_ref, st_ref, cx_ref, cbc_ref, al_ref, db_ref, ds_ref, ng_ref,
    hsend, hrecv, pre, weights, xc, fx, bcv, crecv, dsend, drecv, tot_send, tot_recv,
    edge, erecv, sbuf, srecv, lbuf, ylbuf, tbuf, zrecv, prebuf, pout, pin, gsend, grecv, obuf, szbuf, ysend, yrecv,
    ebuf, yi, sz, gbuf, ssend, ssrecv,
    in_sem, h_sem, d_sem, t_sem, e_sem, c_sem, s_sem, zf_sem, p_sem, g_sem, zb_sem, y_sem, n_sem, near_sem,
):
    seq, tp = lax.axis_index("seq"), lax.axis_index("tp")
    mz, mx = seq // nx, seq % nx
    nseq, ngroups = nz * nx, nz // GROUP
    group, member = mz // GROUP, mz % GROUP
    rows, channels = x_ref.shape
    state = bc_ref.shape[2]
    heads = dt_ref.shape[0]
    quarter = channels // nx
    width = quarter // CHUNKS
    total_width = channels + 2 * state
    part = state // GROUP

    def seq_at(z, x):
        return {"seq": z * nx + x}

    def x_peer(r):
        q = (mx + r) % nx
        return q, seq_at(mz, q)

    def z_peer(r):
        k = (member + r) % GROUP
        return k, seq_at(group * GROUP + k, mx)

    def t_peer(r):
        return {"tp": (tp + r) % ntp}

    following, preceding = {"seq": seq + 1}, {"seq": seq - 1}
    next_group = seq_at(mz + GROUP, mx)

    def remote(src, dst, sem, device):
        return pltpu.make_async_remote_copy(
            src_ref=src, dst_ref=dst, send_sem=sem.at[0], recv_sem=sem.at[1],
            device_id=device, device_id_type=MESH,
        )

    def await_recv(buffer, count, sem):
        some = buffer.at[pl.ds(0, count)]
        remote(some, some, sem, x_peer(1)[1]).wait_recv()

    def await_send(buffer, count, sem):
        some = buffer.at[pl.ds(0, count)]
        remote(some, some, sem, x_peer(1)[1]).wait_send()

    loads = [
        pltpu.make_async_copy(src, dst, in_sem.at[k])
        for k, (src, dst) in enumerate([
            (st_hbm, st_ref), (dt_hbm, dt_ref), (al_hbm, al_ref), (db_hbm, db_ref),
            (x_hbm, x_ref), (bc_hbm, bc_ref), (cx_hbm, cx_ref), (cbc_hbm, cbc_ref),
            (z_hbm, z_ref), (ds_hbm, ds_ref), (ng_hbm, ng_ref),
        ])
    ]
    for load in loads:
        load.start()

    barrier = pltpu.get_barrier_semaphore()

    def greet(device, sem=barrier):
        pl.semaphore_signal(sem, inc=1, device_id=device, device_id_type=MESH)

    def greet_along_z(distance, sem):
        @pl.when(mz >= distance)
        def _():
            greet(seq_at(mz - distance, mx), sem)

        @pl.when(mz + distance < nz)
        def _():
            greet(seq_at(mz + distance, mx), sem)

    def both(distance):
        return (mz >= distance).astype(jnp.int32) + (mz + distance < nz).astype(jnp.int32)

    for r in range(1, nx):
        greet(x_peer(r)[1])
    for r in range(2, GROUP):
        @pl.when(member >= r)
        def _():
            greet(seq_at(mz - r, mx))

        @pl.when(member + r < GROUP)
        def _():
            greet(seq_at(mz + r, mx))

    greet_along_z(1, barrier)

    @pl.when(seq > 0)
    def _():
        greet(preceding)

    for r in range(1, ntp):
        greet(t_peer(r))
    greeted = (nx - 1) + (ntp - 1) + both(1) + (seq + 1 < nseq).astype(jnp.int32)
    for r in range(2, GROUP):
        greeted += (member >= r).astype(jnp.int32) + (member + r < GROUP).astype(jnp.int32)

    row, col = iota((rows, rows), 0), iota((rows, rows), 1)
    tril = (col <= row).astype(F32).astype(BF16)
    ranges = [tril, (col > row).astype(F32).astype(BF16)]
    for d in range(1, REACH + 1):
        ranges.append(((col <= row) & (col > row - d)).astype(F32).astype(BF16))
    spread = iota((heads, channels), 1) // (channels // heads) == iota((heads, channels), 0)
    spread = spread.astype(F32).astype(BF16)
    spread2 = jnp.concatenate([spread, spread], axis=0)
    for load in loads[:4]:
        load.wait()
    starts = jnp.broadcast_to(st_ref[...].astype(F32), (rows, rows)).astype(BF16)
    counts = dot_nt(jnp.concatenate(ranges, axis=0), starts)
    seg_col = counts[:rows]
    to_last = (counts[rows : 2 * rows] == 0.0).astype(F32)
    linked = (seg_col == dot_nt(starts, tril)) & (col <= row)
    from_first = (seg_col == 0.0).astype(F32)
    none_between = [counts[(d + 1) * rows : (d + 2) * rows] == 0.0 for d in range(1, REACH + 1)]
    taps = jnp.concatenate(
        [((col == row - d) & none_between[d - 1]).astype(F32).astype(BF16) for d in range(1, REACH + 1)],
        axis=0,
    )

    for load in loads[4:8]:
        load.wait()
    weights[:, :channels] = cx_ref[...]
    for k in range(REACH + 1):
        weights[k : k + 1, channels : channels + state] = cbc_ref[k, 0:1, :]
        weights[k : k + 1, channels + state :] = cbc_ref[k, 1:2, :]
    b_in, c_in = bc_ref[:, 0, :], bc_ref[:, 1, :]

    tail = slice(rows - 8, rows)
    last_rows = jnp.concatenate(
        [x_ref[tail, :].astype(F32), b_in[tail].astype(F32), c_in[tail].astype(F32)], axis=1
    )
    last_rows = (last_rows * to_last[tail, :1])[8 - FOLD :]
    piece = total_width // FOLD
    hsend[...] = jnp.concatenate(
        [last_rows[:, k * piece : (k + 1) * piece] for k in range(FOLD)], axis=0
    ).astype(BF16)

    def column(ref):
        square = (heads, heads)
        here = iota(square, 0) == iota(square, 1)
        return jnp.sum(jnp.where(here, jnp.broadcast_to(ref[...], square), 0.0), axis=1, keepdims=True)

    raw = dt_ref[...].astype(F32) + column(db_ref)
    step = jnp.maximum(raw, 0.0) + jnp.log1p(jnp.exp(-jnp.abs(raw)))
    decay = -jnp.exp(column(al_ref)) * step
    parts = dot_nt(pieces(decay, 3), tril)
    cumulative = parts[:heads] + parts[heads : 2 * heads] + parts[2 * heads :]
    ebuf[...] = dot_tn(pieces(jnp.exp(cumulative), 2), spread2)
    fall = ebuf[rows - 1 :, :]
    through = fall * (seg_col[rows - 1 : rows, :1] == 0.0).astype(F32)
    for q in range(nx):
        for c in range(CHUNKS):
            at = q * quarter + c * width
            dsend[q, c : c + 1, :] = through[:, at : at + width]
    factor = dot_tn(pieces(jnp.exp(-cumulative) * step, 2), spread2)

    def conv(values, at):
        size = values.shape[1]
        taken = weights[:, at : at + size]
        shifted = dot(taps, values)
        total = taken[REACH:] * values.astype(F32)
        for d in range(1, REACH + 1):
            total += taken[REACH - d : REACH - d + 1] * shifted[(d - 1) * rows : d * rows]
        pre[:, at : at + size] = total[:HEAD]
        return silu(total)

    bcv[:, :state] = conv(b_in, channels).astype(BF16)
    bcv[:, state:] = conv(c_in, channels + state).astype(BF16)
    for at in range(0, channels, 256):
        xc[:, at : at + 256] = conv(x_ref[:, at : at + 256], at).astype(BF16)

    for at in range(0, channels, 256):
        at = slice(at, at + 256)
        fx[:, at] = (xc[:, at].astype(F32) * factor[:, at]).astype(BF16)
    later = to_last * (row >= HEAD).astype(F32)
    bt = jnp.transpose(bcv[:, :state].astype(F32) * later[:, :1]).astype(BF16)
    for c in range(CHUNKS):
        for q in range(nx):
            at = slice(q * quarter + c * width, q * quarter + (c + 1) * width)
            sbuf[c, q] = (dot(bt, fx[:, at]) * fall[:, at]).astype(BF16)

    pl.semaphore_wait(barrier, greeted)

    halo = remote(hsend, hrecv, h_sem, following)

    @pl.when(seq + 1 < nseq)
    def _():
        halo.start()

    greet_along_z(1, near_sem.at[0])
    for r in range(1, nx):
        q, device = x_peer(r)
        remote(dsend.at[q], drecv.at[mx], d_sem, device).start()
    for c in range(CHUNKS):
        for r in range(1, nx):
            q, device = x_peer(r)
            remote(sbuf.at[c, q], srecv.at[c, mx], s_sem.at[c], device).start()
    drecv[mx] = dsend[mx]
    for c in range(CHUNKS):
        srecv[c, mx] = sbuf[c, mx]

    @pl.when(seq == 0)
    def _():
        hrecv[...] = jnp.zeros(hrecv.shape, BF16)

    @pl.when(seq > 0)
    def _():
        halo.wait_recv()

    place_row, place_col = iota((HEAD, HEAD), 0), iota((HEAD, HEAD), 1)
    for k in range(FOLD):
        at = slice(k * piece, (k + 1) * piece)
        reached = []
        for d in range(1, REACH + 1):
            here = (place_col - (k + 1) * FOLD == place_row - d) & (place_row < d)
            here &= none_between[d - 1][:HEAD, :HEAD] & (place_col >= k * FOLD)
            reached.append(here.astype(F32).astype(BF16))
        added = dot(jnp.concatenate(reached, axis=0), hrecv[...])
        total = pre[:, at]
        for d in range(1, REACH + 1):
            total += weights[REACH - d : REACH - d + 1, at] * added[(d - 1) * HEAD : d * HEAD]
        pre[:, at] = total
    done = silu(pre[...]).astype(BF16)
    xc[:HEAD, :] = done[:, :channels]
    bcv[:HEAD, :] = done[:, channels:]
    first_x = done[:, :channels].astype(F32) * factor[:HEAD]
    fx[:HEAD, :] = first_x.astype(BF16)
    first_x = (first_x * fall).astype(BF16)
    first_b = (done[:, channels : channels + state].astype(F32) * to_last[:HEAD, :1]).astype(BF16)
    for q in range(nx):
        edge[q, :, :state] = first_b
        edge[q, :, state:] = first_x[:, q * quarter : (q + 1) * quarter]
    erecv[mx] = edge[mx]
    for r in range(1, nx):
        q, device = x_peer(r)
        remote(edge.at[q], erecv.at[mx], e_sem, device).start()
    b, cc = bcv[:, :state], bcv[:, state:]
    crecv[mx] = cc
    for r in range(1, nx):
        _, device = x_peer(r)
        remote(crecv.at[mx], crecv.at[mx], c_sem, device).start()

    await_recv(drecv, nx - 1, d_sem)
    reach_of = [None, drecv[0]]
    for k in range(1, nx):
        reach_of.append(reach_of[-1] * drecv[k])
    tot_send[...] = reach_of[nx]
    tot_recv[member] = reach_of[nx]
    for r in range(1, GROUP):
        k, device = z_peer(r)
        remote(tot_send, tot_recv.at[member], t_sem, device).start()
    pl.semaphore_wait(near_sem.at[0], both(1))
    if GROUP > 2:
        greet_along_z(2, near_sem.at[1])

    scores = jnp.where(linked, dot_nt(cc, b), 0.0).astype(BF16)
    for q in range(nx):
        at = slice(q * quarter, (q + 1) * quarter)
        yi[:, at] = dot(scores, fx[:, at])
    for load in loads[8:]:
        load.wait()
    sz[...] = silu(z_ref[...].astype(F32))

    if GROUP > 2:
        pl.semaphore_wait(near_sem.at[1], both(2))
    if ngroups > 2:
        @pl.when(group == 2)
        def _():
            greet(seq_at(mz - GROUP, mx), near_sem.at[2])

    await_recv(erecv, nx - 1, e_sem)

    def made(c, k):
        first = dot_tn(erecv[k, :, :state], erecv[k, :, state + c * width : state + (c + 1) * width])
        return srecv[c, k].astype(F32) + first

    for c in range(CHUNKS):
        await_recv(srecv.at[c], nx - 1, s_sem.at[c])
        running = made(c, 0)
        for k in range(1, nx):
            lbuf[c, k - 1] = running.astype(BF16)
            running = drecv[k, c : c + 1, :] * running + made(c, k)
        tbuf[c] = running.astype(BF16).reshape(GROUP, part, width)
        zrecv[c, member] = tbuf[c, member]
        for r in range(1, GROUP):
            k, device = z_peer(r)
            remote(tbuf.at[c, k], zrecv.at[c, member], zf_sem.at[c], device).start()

    await_recv(crecv, nx - 1, c_sem)
    for c in range(CHUNKS):
        for k in range(1, nx):
            ylbuf[c, k - 1] = dot(crecv[k], lbuf[c, k - 1])

    await_recv(tot_recv, GROUP - 1, t_sem)
    row_fall = [tot_recv[k] for k in range(GROUP)]
    group_fall = row_fall[0]
    for k in range(1, GROUP):
        group_fall = row_fall[k] * group_fall
    even = group % 2 == 0
    share_decay = remote(gsend, grecv, g_sem, next_group)

    def hand_on(c, slot, device, sent=0):
        return pltpu.make_async_remote_copy(
            src_ref=pout.at[c], dst_ref=pin.at[c, slot],
            send_sem=p_sem.at[c, sent], recv_sem=p_sem.at[c, 2 + slot],
            device_id=device, device_id_type=MESH,
        )

    after_next_group = seq_at(mz + 2 * GROUP, mx)

    @pl.when(even)
    def _():
        gsend[...] = group_fall
        share_decay.start()
        grecv[...] = jnp.ones(grecv.shape, F32)
        pin[:, 0] = jnp.zeros((CHUNKS, part, width), BF16)

    @pl.when(group < 2)
    def _():
        pin[:, 1] = jnp.zeros((CHUNKS, part, width), BF16)

    group_totals = []
    for c in range(CHUNKS):
        await_recv(zrecv.at[c], GROUP - 1, zf_sem.at[c])
        running = zrecv[c, 0].astype(F32)
        for k in range(1, GROUP):
            prebuf[c, k] = running
            running = row_fall[k][c : c + 1] * running + zrecv[c, k].astype(F32)
        group_totals.append(running)

        @pl.when(even)
        def _():
            pout[c] = running.astype(BF16)
            hand_on(c, 0, next_group).start()

    @pl.when(jnp.logical_not(even))
    def _():
        share_decay.wait_recv()
        for c in range(CHUNKS):
            hand_on(c, 0, next_group).wait_recv()

    if ngroups > 2:
        @pl.when(group == 1)
        def _():
            pl.semaphore_wait(near_sem.at[2], 1)
            for c in range(CHUNKS):
                reached = group_fall[c : c + 1] * pin[c, 0].astype(F32) + group_totals[c]
                pout[c] = reached.astype(BF16)
                hand_on(c, 1, after_next_group, 1).start()
                hand_on(c, 1, next_group).start()

    for c in range(CHUNKS):
        if ngroups > 2:
            @pl.when(group >= 2)
            def _():
                hand_on(c, 1, next_group).wait_recv()

        before = grecv[c : c + 1] * pin[c, 1].astype(F32) + pin[c, 0].astype(F32)
        obuf[c, 0] = before.astype(BF16)
        reach = row_fall[0][c : c + 1]
        for k in range(1, GROUP):
            obuf[c, k] = (reach * before + prebuf[c, k]).astype(BF16)
            reach = row_fall[k][c : c + 1] * reach
        szbuf[c, member] = obuf[c, member]
        for r in range(1, GROUP):
            k, device = z_peer(r)
            remote(obuf.at[c, k], szbuf.at[c, member], zb_sem.at[c], device).start()

    for c in range(CHUNKS):
        await_recv(szbuf.at[c], GROUP - 1, zb_sem.at[c])
        entering = szbuf[c].reshape(state, width)
        for k in range(nx):
            part_y = dot(crecv[k], entering)
            if k:
                part_y = reach_of[k][c : c + 1, :] * part_y + ylbuf[c, k - 1]
            ysend[c, k] = part_y.astype(BF16)
        yrecv[c, mx] = ysend[c, mx]
        for r in range(1, nx):
            q, device = x_peer(r)
            remote(ysend.at[c, q], yrecv.at[c, mx], y_sem.at[c], device).start()

    skip = dot_tn(pieces(jnp.broadcast_to(column(ds_ref), (heads, 128)), 2), spread2)[:1]
    squares = jnp.zeros((rows, 128), F32)
    for c in range(CHUNKS):
        await_recv(yrecv.at[c], nx - 1, y_sem.at[c])
        for q in range(nx):
            at = slice(q * quarter + c * width, q * quarter + (c + 1) * width)
            y = yi[:, at] + from_first[:, :1] * yrecv[c, q].astype(F32)
            y = ebuf[:, at] * y + skip[:, at] * xc[:, at].astype(F32)
            gated = y * sz[:, at]
            gbuf[:, at] = gated
            for k in range(0, width, 128):
                some = gated[:, k : k + 128]
                squares += some * some
    total = jnp.sum(jnp.transpose(squares), axis=0, keepdims=True)
    total = jnp.broadcast_to(total, ssend.shape)
    ssend[...] = total
    ssrecv[tp] = total
    for r in range(1, ntp):
        remote(ssend, ssrecv.at[tp], n_sem, t_peer(r)).start()
    await_recv(ssrecv, ntp - 1, n_sem)
    total = jnp.sum(ssrecv[...], axis=0)[:1]
    inverse = lax.rsqrt(total / (channels * ntp) + EPSILON)
    inverse = jnp.transpose(jnp.broadcast_to(inverse, (rows, rows)))
    for at in range(0, channels, 128):
        at = slice(at, at + 128)
        out_ref[:, at] = (gbuf[:, at] * inverse * ng_ref[:, at]).astype(BF16)

    @pl.when(seq + 1 < nseq)
    def _():
        halo.wait_send()

    await_send(drecv, nx - 1, d_sem)
    await_send(tot_recv, GROUP - 1, t_sem)
    await_send(erecv, nx - 1, e_sem)
    await_send(crecv, nx - 1, c_sem)
    for c in range(CHUNKS):
        await_send(srecv.at[c], nx - 1, s_sem.at[c])
        await_send(zrecv.at[c], GROUP - 1, zf_sem.at[c])

        @pl.when(even)
        def _():
            if c == 0:
                share_decay.wait_send()
            hand_on(c, 0, next_group).wait_send()

        if ngroups > 2:
            @pl.when(group == 1)
            def _():
                hand_on(c, 1, next_group).wait_send()
                hand_on(c, 1, after_next_group, 1).wait_send()

        await_send(szbuf.at[c], GROUP - 1, zb_sem.at[c])
        await_send(yrecv.at[c], nx - 1, y_sem.at[c])
    await_send(ssrecv, ntp - 1, n_sem)


def per_device(
    x_in, bc_in, z_in, dt_raw, starts, conv_x, conv_bc, a_log, dt_bias, d_skip, norm_gain
):
    rows, channels = x_in.shape
    state = bc_in.shape[2]
    heads = dt_raw.shape[1]
    nx, ntp = NX, lax.axis_size("tp")
    nz = lax.axis_size("seq") // nx
    width = channels // nx // CHUNKS
    total_width = channels + 2 * state
    part = state // GROUP
    operands = (
        x_in,
        bc_in,
        z_in,
        dt_raw.T,
        starts.reshape(1, rows),
        conv_x,
        conv_bc,
        a_log.reshape(1, heads),
        dt_bias.reshape(1, heads),
        d_skip.reshape(1, heads),
        norm_gain.reshape(1, channels),
    )
    operands = tuple(pltpu.with_memory_space_constraint(o, pltpu.HBM) for o in operands)
    sems = pltpu.SemaphoreType.DMA
    return pl.pallas_call(
        functools.partial(kernel, nz, nx, ntp),
        out_shape=jax.ShapeDtypeStruct((rows, channels), BF16),
        in_specs=[pl.BlockSpec(memory_space=pltpu.HBM)] * len(operands),
        out_specs=pl.BlockSpec(memory_space=pltpu.VMEM),
        scratch_shapes=[
            *(pltpu.VMEM(operand.shape, operand.dtype) for operand in operands),
            pltpu.VMEM((4 * FOLD, total_width // FOLD), BF16),
            pltpu.VMEM((4 * FOLD, total_width // FOLD), BF16),
            pltpu.VMEM((HEAD, total_width), F32),
            pltpu.VMEM((REACH + 1, total_width), F32),
            pltpu.VMEM((rows, channels), BF16),
            pltpu.VMEM((rows, channels), BF16),
            pltpu.VMEM((rows, 2 * state), BF16),
            pltpu.VMEM((nx, rows, state), BF16),
            pltpu.VMEM((nx, CHUNKS, width), F32),
            pltpu.VMEM((nx, CHUNKS, width), F32),
            pltpu.VMEM((CHUNKS, width), F32),
            pltpu.VMEM((GROUP, CHUNKS, width), F32),
            pltpu.VMEM((nx, HEAD, state + width * CHUNKS), BF16),
            pltpu.VMEM((nx, HEAD, state + width * CHUNKS), BF16),
            pltpu.VMEM((CHUNKS, nx, state, width), BF16),
            pltpu.VMEM((CHUNKS, nx, state, width), BF16),
            pltpu.VMEM((CHUNKS, nx - 1, state, width), BF16),
            pltpu.VMEM((CHUNKS, nx - 1, rows, width), F32),
            pltpu.VMEM((CHUNKS, GROUP, part, width), BF16),
            pltpu.VMEM((CHUNKS, GROUP, part, width), BF16),
            pltpu.VMEM((CHUNKS, GROUP, part, width), F32),
            pltpu.VMEM((CHUNKS, part, width), BF16),
            pltpu.VMEM((CHUNKS, 2, part, width), BF16),
            pltpu.VMEM((CHUNKS, width), F32),
            pltpu.VMEM((CHUNKS, width), F32),
            pltpu.VMEM((CHUNKS, GROUP, part, width), BF16),
            pltpu.VMEM((CHUNKS, GROUP, part, width), BF16),
            pltpu.VMEM((CHUNKS, nx, rows, width), BF16),
            pltpu.VMEM((CHUNKS, nx, rows, width), BF16),
            pltpu.VMEM((rows, channels), F32),
            pltpu.VMEM((rows, channels), F32),
            pltpu.VMEM((rows, channels), F32),
            pltpu.VMEM((rows, channels), F32),
            pltpu.VMEM((1, 128), F32),
            pltpu.VMEM((ntp, 1, 128), F32),
            sems((len(operands),)),
            sems((2,)),
            sems((2,)),
            sems((2,)),
            sems((2,)),
            sems((2,)),
            sems((CHUNKS, 2)),
            sems((CHUNKS, 2)),
            sems((CHUNKS, 4)),
            sems((2,)),
            sems((CHUNKS, 2)),
            sems((CHUNKS, 2)),
            sems((2,)),
            pltpu.SemaphoreType.REGULAR((3,)),
        ],
        compiler_params=pltpu.CompilerParams(
            collective_id=0, has_side_effects=True, vmem_limit_bytes=40 * 2**20
        ),
        cost_estimate=pl.CostEstimate(flops=2 * 10**8, bytes_accessed=2**20, transcendentals=10**6),
    )(*operands)


def solution(mesh):
    return jax.shard_map(
        per_device,
        mesh=mesh,
        in_specs=(
            P("seq", "tp"),
            P("seq", None, "tp"),
            P("seq", "tp"),
            P("seq", "tp"),
            P("seq"),
            P(None, "tp"),
            P(None, None, "tp"),
            P("tp"),
            P("tp"),
            P("tp"),
            P("tp"),
        ),
        out_specs=P("seq", "tp"),
        check_vma=False,
    )
```

profile of v0, /device:TPU:480, one launch (start us, length us, event | category | flops | bytes accessed | tf_op | source)
XLA Modules:
  0.0 40.8 jit_solution(14032246036185150759)
XLA Ops:
  0.0 40.0 %shard_map.109 = bf16[128,1024]{1,0:T(8,128)(2,1)S(1)} custom-call(bf16[128,1024]{1,0:T(8,128)(2,1)} %x_hbm.1, bf16[128,2,256]{2,1,0:T(2,128)(2,1)} %bc_hbm.1, bf16[128,1024]{1,0:T(8,128)(2,1)} %z_hbm.1, bf16[16,128]{1,0:T(8,128)(2,1)} %bitcast.6, s32[1,128]{1,0:T(1,128)} %bitcast.8, f32[4,1024]{1,0:T(4,128)} %cx_hbm.1, f32[4,2,256]{2,1,0:T(2,128)} %cbc_hbm.1, ...), custom_call_target="tpu_custom_call" | custom-call | flops 200000000 | bytes 1048576 | tf_op jit(solution)/shard_map/pallas_call | solution.py:520
  40.0 0.7 %copy.13 = bf16[128,1024]{1,0:T(8,128)(2,1)} copy(bf16[128,1024]{1,0:T(8,128)(2,1)S(1)} %shard_map.109) | data formatting | bytes 524288
where the time goes:
time: 41.2 us; the launch traced here: 40.8 us
  Pallas kernels  40 us (97%)
  local copies, waits for them, and re-layouts  0.71 us (2%)
    pallas_call x1, Pallas kernels, per_device(): pl.pallas_call(functools.partial(kernel, nz, nx, ntp), out_shape=jax.Shap...  40 us

commit v1 on v0

--- a/solution.py
+++ b/solution.py
@@ -235,6 +235,16 @@
             at = slice(q * quarter + c * width, q * quarter + (c + 1) * width)
             sbuf[c, q] = (dot(bt, fx[:, at]) * fall[:, at]).astype(BF16)
 
+    place_row, place_col = iota((HEAD, HEAD), 0), iota((HEAD, HEAD), 1)
+    reached = []
+    for k in range(FOLD):
+        matrices = []
+        for d in range(1, REACH + 1):
+            here = (place_col - (k + 1) * FOLD == place_row - d) & (place_row < d)
+            here &= none_between[d - 1][:HEAD, :HEAD] & (place_col >= k * FOLD)
+            matrices.append(here.astype(F32).astype(BF16))
+        reached.append(jnp.concatenate(matrices, axis=0))
+
     pl.semaphore_wait(barrier, greeted)
 
     halo = remote(hsend, hrecv, h_sem, following)
@@ -247,10 +257,12 @@
     for r in range(1, nx):
         q, device = x_peer(r)
         remote(dsend.at[q], drecv.at[mx], d_sem, device).start()
-    for c in range(CHUNKS):
-        for r in range(1, nx):
+    def send_states(c):
+        for r in (2, 1, 3) if nx == 4 else range(1, nx):
             q, device = x_peer(r)
             remote(sbuf.at[c, q], srecv.at[c, mx], s_sem.at[c], device).start()
+
+    send_states(0)
     drecv[mx] = dsend[mx]
     for c in range(CHUNKS):
         srecv[c, mx] = sbuf[c, mx]
@@ -263,15 +275,9 @@
     def _():
         halo.wait_recv()
 
-    place_row, place_col = iota((HEAD, HEAD), 0), iota((HEAD, HEAD), 1)
     for k in range(FOLD):
         at = slice(k * piece, (k + 1) * piece)
-        reached = []
-        for d in range(1, REACH + 1):
-            here = (place_col - (k + 1) * FOLD == place_row - d) & (place_row < d)
-            here &= none_between[d - 1][:HEAD, :HEAD] & (place_col >= k * FOLD)
-            reached.append(here.astype(F32).astype(BF16))
-        added = dot(jnp.concatenate(reached, axis=0), hrecv[...])
+        added = dot(reached[k], hrecv[...])
         total = pre[:, at]
         for d in range(1, REACH + 1):
             total += weights[REACH - d : REACH - d + 1, at] * added[(d - 1) * HEAD : d * HEAD]
@@ -290,11 +296,10 @@
     for r in range(1, nx):
         q, device = x_peer(r)
         remote(edge.at[q], erecv.at[mx], e_sem, device).start()
+    for c in range(1, CHUNKS):
+        send_states(c)
     b, cc = bcv[:, :state], bcv[:, state:]
     crecv[mx] = cc
-    for r in range(1, nx):
-        _, device = x_peer(r)
-        remote(crecv.at[mx], crecv.at[mx], c_sem, device).start()
 
     await_recv(drecv, nx - 1, d_sem)
     reach_of = [None, drecv[0]]
@@ -310,12 +315,15 @@
         greet_along_z(2, near_sem.at[1])
 
     scores = jnp.where(linked, dot_nt(cc, b), 0.0).astype(BF16)
+    for load in loads[8:]:
+        load.wait()
+    skip = dot_tn(pieces(jnp.broadcast_to(column(ds_ref), (heads, 128)), 2), spread2)[:1]
     for q in range(nx):
         at = slice(q * quarter, (q + 1) * quarter)
-        yi[:, at] = dot(scores, fx[:, at])
-    for load in loads[8:]:
-        load.wait()
-    sz[...] = silu(z_ref[...].astype(F32))
+        gate = silu(z_ref[:, at].astype(F32))
+        own = ebuf[:, at] * dot(scores, fx[:, at]) + skip[:, at] * xc[:, at].astype(F32)
+        yi[:, at] = own * gate
+        sz[:, at] = ebuf[:, at] * from_first[:, :1] * gate
 
     if GROUP > 2:
         pl.semaphore_wait(near_sem.at[1], both(2))
@@ -342,10 +350,9 @@
             k, device = z_peer(r)
             remote(tbuf.at[c, k], zrecv.at[c, member], zf_sem.at[c], device).start()
 
-    await_recv(crecv, nx - 1, c_sem)
-    for c in range(CHUNKS):
-        for k in range(1, nx):
-            ylbuf[c, k - 1] = dot(crecv[k], lbuf[c, k - 1])
+    for r in range(1, nx):
+        _, device = x_peer(r)
+        remote(crecv.at[mx], crecv.at[mx], c_sem, device).start()
 
     await_recv(tot_recv, GROUP - 1, t_sem)
     row_fall = [tot_recv[k] for k in range(GROUP)]
@@ -421,6 +428,11 @@
         for r in range(1, GROUP):
             k, device = z_peer(r)
             remote(obuf.at[c, k], szbuf.at[c, member], zb_sem.at[c], device).start()
+
+    await_recv(crecv, nx - 1, c_sem)
+    for c in range(CHUNKS):
+        for k in range(1, nx):
+            ylbuf[c, k - 1] = dot(crecv[k], lbuf[c, k - 1])
 
     for c in range(CHUNKS):
         await_recv(szbuf.at[c], GROUP - 1, zb_sem.at[c])
@@ -435,15 +447,12 @@
             q, device = x_peer(r)
             remote(ysend.at[c, q], yrecv.at[c, mx], y_sem.at[c], device).start()
 
-    skip = dot_tn(pieces(jnp.broadcast_to(column(ds_ref), (heads, 128)), 2), spread2)[:1]
     squares = jnp.zeros((rows, 128), F32)
     for c in range(CHUNKS):
         await_recv(yrecv.at[c], nx - 1, y_sem.at[c])
         for q in range(nx):
             at = slice(q * quarter + c * width, q * quarter + (c + 1) * width)
-            y = yi[:, at] + from_first[:, :1] * yrecv[c, q].astype(F32)
-            y = ebuf[:, at] * y + skip[:, at] * xc[:, at].astype(F32)
-            gated = y * sz[:, at]
+            gated = yi[:, at] + sz[:, at] * yrecv[c, q].astype(F32)
             gbuf[:, at] = gated
             for k in range(0, width, 128):
                 some = gated[:, k : k + 128]

time: 41.2 us -> 40.3 us (0.978)
  Pallas kernels: 40 us -> 39.4 us
    pallas_call x1, Pallas kernels: 40 us -> 39.4 us  [per_device(): pl.pallas_call(functools.partial(kernel, nz, nx, ntp), out_shape=jax.Shap...]
where the time goes in v1:
time: 40.3 us; the launch traced here: 40.1 us
  Pallas kernels  39.4 us (98%)
  local copies, waits for them, and re-layouts  0.71 us (2%)
    pallas_call x1, Pallas kernels, per_device(): pl.pallas_call(functools.partial(kernel, nz, nx, ntp), out_shape=jax.Shap...  39.4 us

profile of v1, /device:TPU:480, one launch (start us, length us, event | category | flops | bytes accessed | tf_op | source)
XLA Modules:
  0.0 40.1 jit_solution(11919510627429097263)
XLA Ops:
  0.0 39.4 %shard_map.109 = bf16[128,1024]{1,0:T(8,128)(2,1)S(1)} custom-call(bf16[128,1024]{1,0:T(8,128)(2,1)} %x_hbm.1, bf16[128,2,256]{2,1,0:T(2,128)(2,1)} %bc_hbm.1, bf16[128,1024]{1,0:T(8,128)(2,1)} %z_hbm.1, bf16[16,128]{1,0:T(8,128)(2,1)} %bitcast.6, s32[1,128]{1,0:T(1,128)} %bitcast.8, f32[4,1024]{1,0:T(4,128)} %cx_hbm.1, f32[4,2,256]{2,1,0:T(2,128)} %cbc_hbm.1, ...), custom_call_target="tpu_custom_call" | custom-call | flops 200000000 | bytes 1048576 | tf_op jit(solution)/shard_map/pallas_call | solution.py:529
  39.4 0.7 %copy.13 = bf16[128,1024]{1,0:T(8,128)(2,1)} copy(bf16[128,1024]{1,0:T(8,128)(2,1)S(1)} %shard_map.109) | data formatting | bytes 524288

commit v2 on v1

--- a/solution.py
+++ b/solution.py
@@ -84,7 +84,14 @@
         return {"tp": (tp + r) % ntp}
 
     following, preceding = {"seq": seq + 1}, {"seq": seq - 1}
-    next_group = seq_at(mz + GROUP, mx)
+    swap = 1 - 2 * (member % 2)
+    swapped = (group == ngroups - 1).astype(jnp.int32) * (ngroups > 2)
+    to_swapped = (group == ngroups - 2).astype(jnp.int32) * (ngroups > 2)
+    next_group = seq_at(mz + GROUP + to_swapped * swap, mx)
+
+    def slice_of(k):
+        return k + swapped * (1 - 2 * (k % 2))
+
 
     def remote(src, dst, sem, device):
         return pltpu.make_async_remote_copy(
@@ -116,30 +123,21 @@
     def greet(device, sem=barrier):
         pl.semaphore_signal(sem, inc=1, device_id=device, device_id_type=MESH)
 
-    def greet_along_z(distance, sem):
-        @pl.when(mz >= distance)
-        def _():
-            greet(seq_at(mz - distance, mx), sem)
-
-        @pl.when(mz + distance < nz)
-        def _():
-            greet(seq_at(mz + distance, mx), sem)
-
-    def both(distance):
-        return (mz >= distance).astype(jnp.int32) + (mz + distance < nz).astype(jnp.int32)
-
     for r in range(1, nx):
         greet(x_peer(r)[1])
-    for r in range(2, GROUP):
-        @pl.when(member >= r)
-        def _():
-            greet(seq_at(mz - r, mx))
-
-        @pl.when(member + r < GROUP)
-        def _():
-            greet(seq_at(mz + r, mx))
-
-    greet_along_z(1, barrier)
+    for r in range(1, GROUP):
+        greet(z_peer(r)[1])
+
+    first, last = member == 0, member == GROUP - 1
+    below, above = group > 0, group + 1 < ngroups
+
+    @pl.when(last & above)
+    def _():
+        greet(seq_at(mz + 1, mx))
+
+    def greet_group(sem):
+        for r in range(1, GROUP):
+            greet(z_peer(r)[1], sem)
 
     @pl.when(seq > 0)
     def _():
@@ -147,9 +145,8 @@
 
     for r in range(1, ntp):
         greet(t_peer(r))
-    greeted = (nx - 1) + (ntp - 1) + both(1) + (seq + 1 < nseq).astype(jnp.int32)
-    for r in range(2, GROUP):
-        greeted += (member >= r).astype(jnp.int32) + (member + r < GROUP).astype(jnp.int32)
+    greeted = (nx - 1) + (GROUP - 1) + (ntp - 1)
+    greeted += (seq + 1 < nseq).astype(jnp.int32) + (first & below).astype(jnp.int32)
 
     row, col = iota((rows, rows), 0), iota((rows, rows), 1)
     tril = (col <= row).astype(F32).astype(BF16)
@@ -253,7 +250,10 @@
     def _():
         halo.start()
 
-    greet_along_z(1, near_sem.at[0])
+    @pl.when(first & below)
+    def _():
+        greet(seq_at(mz - 1, mx), near_sem.at[0])
+
     for r in range(1, nx):
         q, device = x_peer(r)
         remote(dsend.at[q], drecv.at[mx], d_sem, device).start()
@@ -310,9 +310,10 @@
     for r in range(1, GROUP):
         k, device = z_peer(r)
         remote(tot_send, tot_recv.at[member], t_sem, device).start()
-    pl.semaphore_wait(near_sem.at[0], both(1))
-    if GROUP > 2:
-        greet_along_z(2, near_sem.at[1])
+    @pl.when(last & above)
+    def _():
+        pl.semaphore_wait(near_sem.at[0], 1)
+        greet_group(near_sem.at[1])
 
     scores = jnp.where(linked, dot_nt(cc, b), 0.0).astype(BF16)
     for load in loads[8:]:
@@ -325,13 +326,6 @@
         yi[:, at] = own * gate
         sz[:, at] = ebuf[:, at] * from_first[:, :1] * gate
 
-    if GROUP > 2:
-        pl.semaphore_wait(near_sem.at[1], both(2))
-    if ngroups > 2:
-        @pl.when(group == 2)
-        def _():
-            greet(seq_at(mz - GROUP, mx), near_sem.at[2])
-
     await_recv(erecv, nx - 1, e_sem)
 
     def made(c, k):
@@ -345,14 +339,28 @@
             lbuf[c, k - 1] = running.astype(BF16)
             running = drecv[k, c : c + 1, :] * running + made(c, k)
         tbuf[c] = running.astype(BF16).reshape(GROUP, part, width)
-        zrecv[c, member] = tbuf[c, member]
+        zrecv[c, member] = tbuf[c, slice_of(member)]
         for r in range(1, GROUP):
             k, device = z_peer(r)
-            remote(tbuf.at[c, k], zrecv.at[c, member], zf_sem.at[c], device).start()
+            remote(tbuf.at[c, slice_of(k)], zrecv.at[c, member], zf_sem.at[c], device).start()
 
     for r in range(1, nx):
         _, device = x_peer(r)
         remote(crecv.at[mx], crecv.at[mx], c_sem, device).start()
+
+    @pl.when(jnp.logical_not(last) & above)
+    def _():
+        pl.semaphore_wait(near_sem.at[1], 1)
+
+    if ngroups > 2:
+        @pl.when(first & (group == 2))
+        def _():
+            greet(seq_at(mz - 1, mx), near_sem.at[2])
+
+        @pl.when(last & (group == 1))
+        def _():
+            pl.semaphore_wait(near_sem.at[2], 1)
+            greet_group(near_sem.at[3])
 
     await_recv(tot_recv, GROUP - 1, t_sem)
     row_fall = [tot_recv[k] for k in range(GROUP)]
@@ -369,7 +377,7 @@
             device_id=device, device_id_type=MESH,
         )
 
-    after_next_group = seq_at(mz + 2 * GROUP, mx)
+    after_next_group = seq_at(mz + 2 * GROUP + swap, mx)
 
     @pl.when(even)
     def _():
@@ -405,7 +413,10 @@
     if ngroups > 2:
         @pl.when(group == 1)
         def _():
-            pl.semaphore_wait(near_sem.at[2], 1)
+            @pl.when(jnp.logical_not(last))
+            def _():
+                pl.semaphore_wait(near_sem.at[3], 1)
+
             for c in range(CHUNKS):
                 reached = group_fall[c : c + 1] * pin[c, 0].astype(F32) + group_totals[c]
                 pout[c] = reached.astype(BF16)
@@ -424,10 +435,10 @@
         for k in range(1, GROUP):
             obuf[c, k] = (reach * before + prebuf[c, k]).astype(BF16)
             reach = row_fall[k][c : c + 1] * reach
-        szbuf[c, member] = obuf[c, member]
+        szbuf[c, slice_of(member)] = obuf[c, member]
         for r in range(1, GROUP):
             k, device = z_peer(r)
-            remote(obuf.at[c, k], szbuf.at[c, member], zb_sem.at[c], device).start()
+            remote(obuf.at[c, k], szbuf.at[c, slice_of(member)], zb_sem.at[c], device).start()
 
     await_recv(crecv, nx - 1, c_sem)
     for c in range(CHUNKS):
@@ -581,7 +592,7 @@
             sems((CHUNKS, 2)),
             sems((CHUNKS, 2)),
             sems((2,)),
-            pltpu.SemaphoreType.REGULAR((3,)),
+            pltpu.SemaphoreType.REGULAR((4,)),
         ],
         compiler_params=pltpu.CompilerParams(
             collective_id=0, has_side_effects=True, vmem_limit_bytes=40 * 2**20

time: 40.3 us -> 39.5 us (0.980)
  Pallas kernels: 39.4 us -> 38.6 us
    pallas_call x1, Pallas kernels: 39.4 us -> 38.6 us  [per_device(): pl.pallas_call(functools.partial(kernel, nz, nx, ntp), out_shape=jax.Shap...]
where the time goes in v2:
time: 39.5 us; the launch traced here: 39.3 us
  Pallas kernels  38.6 us (98%)
  local copies, waits for them, and re-layouts  0.71 us (2%)
    pallas_call x1, Pallas kernels, per_device(): pl.pallas_call(functools.partial(kernel, nz, nx, ntp), out_shape=jax.Shap...  38.6 us

profile of v2, /device:TPU:480, one launch (start us, length us, event | category | flops | bytes accessed | tf_op | source)
XLA Modules:
  0.0 39.3 jit_solution(17719915868284556365)
XLA Ops:
  0.0 38.6 %shard_map.109 = bf16[128,1024]{1,0:T(8,128)(2,1)S(1)} custom-call(bf16[128,1024]{1,0:T(8,128)(2,1)} %x_hbm.1, bf16[128,2,256]{2,1,0:T(2,128)(2,1)} %bc_hbm.1, bf16[128,1024]{1,0:T(8,128)(2,1)} %z_hbm.1, bf16[16,128]{1,0:T(8,128)(2,1)} %bitcast.6, s32[1,128]{1,0:T(1,128)} %bitcast.8, f32[4,1024]{1,0:T(4,128)} %cx_hbm.1, f32[4,2,256]{2,1,0:T(2,128)} %cbc_hbm.1, ...), custom_call_target="tpu_custom_call" | custom-call | flops 200000000 | bytes 1048576 | tf_op jit(solution)/shard_map/pallas_call | solution.py:540
  38.6 0.7 %copy.13 = bf16[128,1024]{1,0:T(8,128)(2,1)} copy(bf16[128,1024]{1,0:T(8,128)(2,1)S(1)} %shard_map.109) | data formatting | bytes 524288

commit v3 on v2

--- a/solution.py
+++ b/solution.py
@@ -390,40 +390,41 @@
     def _():
         pin[:, 1] = jnp.zeros((CHUNKS, part, width), BF16)
 
-    group_totals = []
     for c in range(CHUNKS):
         await_recv(zrecv.at[c], GROUP - 1, zf_sem.at[c])
         running = zrecv[c, 0].astype(F32)
         for k in range(1, GROUP):
             prebuf[c, k] = running
             running = row_fall[k][c : c + 1] * running + zrecv[c, k].astype(F32)
-        group_totals.append(running)
 
         @pl.when(even)
         def _():
             pout[c] = running.astype(BF16)
             hand_on(c, 0, next_group).start()
 
-    @pl.when(jnp.logical_not(even))
-    def _():
-        share_decay.wait_recv()
-        for c in range(CHUNKS):
-            hand_on(c, 0, next_group).wait_recv()
-
-    if ngroups > 2:
-        @pl.when(group == 1)
-        def _():
-            @pl.when(jnp.logical_not(last))
+        if ngroups > 2:
+            @pl.when(group == 1)
             def _():
-                pl.semaphore_wait(near_sem.at[3], 1)
-
-            for c in range(CHUNKS):
-                reached = group_fall[c : c + 1] * pin[c, 0].astype(F32) + group_totals[c]
+                if c == 0:
+                    @pl.when(jnp.logical_not(last))
+                    def _():
+                        pl.semaphore_wait(near_sem.at[3], 1)
+
+                hand_on(c, 0, next_group).wait_recv()
+                reached = group_fall[c : c + 1] * pin[c, 0].astype(F32) + running
                 pout[c] = reached.astype(BF16)
                 hand_on(c, 1, after_next_group, 1).start()
                 hand_on(c, 1, next_group).start()
 
-    for c in range(CHUNKS):
+    @pl.when(jnp.logical_not(even))
+    def _():
+        share_decay.wait_recv()
+
+    for c in range(CHUNKS):
+        @pl.when(jnp.logical_not(even) & ((group != 1) | (ngroups <= 2)))
+        def _():
+            hand_on(c, 0, next_group).wait_recv()
+
         if ngroups > 2:
             @pl.when(group >= 2)
             def _():
@@ -448,8 +449,9 @@
     for c in range(CHUNKS):
         await_recv(szbuf.at[c], GROUP - 1, zb_sem.at[c])
         entering = szbuf[c].reshape(state, width)
+        all_y = dot(crecv[...].reshape(nx * rows, state), entering)
         for k in range(nx):
-            part_y = dot(crecv[k], entering)
+            part_y = all_y[k * rows : (k + 1) * rows]
             if k:
                 part_y = reach_of[k][c : c + 1, :] * part_y + ylbuf[c, k - 1]
             ysend[c, k] = part_y.astype(BF16)

time: 39.5 us -> 39.5 us (level)
  no operation moved by 1% of the time
where the time goes in v3:
time: 39.5 us; the launch traced here: 39.4 us
  Pallas kernels  38.7 us (98%)
  local copies, waits for them, and re-layouts  0.71 us (2%)
    pallas_call x1, Pallas kernels, per_device(): pl.pallas_call(functools.partial(kernel, nz, nx, ntp), out_shape=jax.Shap...  38.7 us

profile of v3, /device:TPU:480, one launch (start us, length us, event | category | flops | bytes accessed | tf_op | source)
XLA Modules:
  0.0 39.4 jit_solution(2201285953495064069)
XLA Ops:
  0.0 38.7 %shard_map.109 = bf16[128,1024]{1,0:T(8,128)(2,1)S(1)} custom-call(bf16[128,1024]{1,0:T(8,128)(2,1)} %x_hbm.1, bf16[128,2,256]{2,1,0:T(2,128)(2,1)} %bc_hbm.1, bf16[128,1024]{1,0:T(8,128)(2,1)} %z_hbm.1, bf16[16,128]{1,0:T(8,128)(2,1)} %bitcast.6, s32[1,128]{1,0:T(1,128)} %bitcast.8, f32[4,1024]{1,0:T(4,128)} %cx_hbm.1, f32[4,2,256]{2,1,0:T(2,128)} %cbc_hbm.1, ...), custom_call_target="tpu_custom_call" | custom-call | flops 200000000 | bytes 1048576 | tf_op jit(solution)/shard_map/pallas_call | solution.py:542
  38.7 0.7 %copy.13 = bf16[128,1024]{1,0:T(8,128)(2,1)} copy(bf16[128,1024]{1,0:T(8,128)(2,1)S(1)} %shard_map.109) | data formatting | bytes 524288

commit v4 on v2

--- a/solution.py
+++ b/solution.py
@@ -474,13 +474,14 @@
     ssrecv[tp] = total
     for r in range(1, ntp):
         remote(ssend, ssrecv.at[tp], n_sem, t_peer(r)).start()
+    gbuf[...] = gbuf[...] * ng_ref[...]
     await_recv(ssrecv, ntp - 1, n_sem)
     total = jnp.sum(ssrecv[...], axis=0)[:1]
     inverse = lax.rsqrt(total / (channels * ntp) + EPSILON)
     inverse = jnp.transpose(jnp.broadcast_to(inverse, (rows, rows)))
     for at in range(0, channels, 128):
         at = slice(at, at + 128)
-        out_ref[:, at] = (gbuf[:, at] * inverse * ng_ref[:, at]).astype(BF16)
+        out_ref[:, at] = (gbuf[:, at] * inverse).astype(BF16)
 
     @pl.when(seq + 1 < nseq)
     def _():

time: 39.5 us -> 39.5 us (level)
  no operation moved by 1% of the time
where the time goes in v4:
time: 39.5 us; the launch traced here: 39.3 us
  Pallas kernels  38.6 us (98%)
  local copies, waits for them, and re-layouts  0.71 us (2%)
    pallas_call x1, Pallas kernels, per_device(): pl.pallas_call(functools.partial(kernel, nz, nx, ntp), out_shape=jax.Shap...  38.6 us

profile of v4, /device:TPU:480, one launch (start us, length us, event | category | flops | bytes accessed | tf_op | source)
XLA Modules:
  0.0 39.3 jit_solution(13852327605140184711)
XLA Ops:
  0.0 38.6 %shard_map.109 = bf16[128,1024]{1,0:T(8,128)(2,1)S(1)} custom-call(bf16[128,1024]{1,0:T(8,128)(2,1)} %x_hbm.1, bf16[128,2,256]{2,1,0:T(2,128)(2,1)} %bc_hbm.1, bf16[128,1024]{1,0:T(8,128)(2,1)} %z_hbm.1, bf16[16,128]{1,0:T(8,128)(2,1)} %bitcast.6, s32[1,128]{1,0:T(1,128)} %bitcast.8, f32[4,1024]{1,0:T(4,128)} %cx_hbm.1, f32[4,2,256]{2,1,0:T(2,128)} %cbc_hbm.1, ...), custom_call_target="tpu_custom_call" | custom-call | flops 200000000 | bytes 1048576 | tf_op jit(solution)/shard_map/pallas_call | solution.py:541
  38.6 0.7 %copy.13 = bf16[128,1024]{1,0:T(8,128)(2,1)} copy(bf16[128,1024]{1,0:T(8,128)(2,1)S(1)} %shard_map.109) | data formatting | bytes 524288
